TPU v7x, 32 devices: a whole 2x2x4 slice. The times are simulated.
32 devices in a mesh: lat: 4 (over y, x), lon: 8 (over z, core).
Axes of the slice: x: 2, y: 2, z: 4, core: 2. Of those that a mesh axis runs over, the one named last changes fastest.
Arguments:
- query_tok: bfloat16 [32, 128, 1536], P('lat', 'lon'), may hold values from -9 to 9
- key_tok: bfloat16 [32, 128, 1536], P('lat', 'lon'), may hold values from -9 to 9
- value_tok: bfloat16 [32, 128, 1536], P('lat', 'lon'), may hold values from -6 to 6
- query_tan: bfloat16 [32, 128, 1536], P('lat', 'lon'), may hold values from -6 to 6
- key_tan: bfloat16 [32, 128, 1536], P('lat', 'lon'), may hold values from -6 to 6
- value_tan: bfloat16 [32, 128, 1536], P('lat', 'lon'), may hold values from -6 to 6
Outputs:
- attended: bfloat16 [32, 128, 1536], P('lat', 'lon')
- attended_tan: bfloat16 [32, 128, 1536], P('lat', 'lon')
All inputs are finite; a program needn't handle non-finite values.
Results may differ from a plain program's by a relative error of at most 0.012.
The roundings to bfloat16 on the way count: a program that leaves them out, or rounds other values in their place, can miss the bound.
Values may be sent and summed in bfloat16 or wider, within the bound.
A program may use at most 64 MiB of HBM per device.

v0:
```python
import functools
import math

import jax
import jax.numpy as jnp
import numpy as np
from jax import lax
from jax.experimental import pallas as pl
from jax.experimental.pallas import tpu as pltpu
from jax.sharding import PartitionSpec as P

HD = 128
WIN = 16


def extended_2(shard, sides, width, wrap):
    for axis, dim in sides:
        count, length = (lax.axis_size(axis), shard.shape[dim])
        up = [(i, (i + 1) % count) for i in range(count if wrap else count - 1)]
        down = [(j, i) for i, j in up]
        last = lax.slice_in_dim(shard, length - width, length, axis=dim)
        leading = lax.slice_in_dim(shard, 0, width, axis=dim)
        before = lax.ppermute(last, axis, up)
        after = lax.ppermute(leading, axis, down)
        shard = jnp.concatenate([before, shard, after], axis=dim)
    return shard


def rotate_rays(values, row_first, col_first, total_rows, total_cols):
    band_rows, sector_cols, feature_width = values.shape
    quarter = HD // 4
    head_count = feature_width // HD
    frequency = (jnp.arange(quarter, dtype=jnp.int32) + 1).astype(jnp.float32)
    row_ids = (row_first + jnp.arange(band_rows, dtype=jnp.int32)).astype(jnp.float32)
    col_ids = (col_first + jnp.arange(sector_cols, dtype=jnp.int32)).astype(jnp.float32)
    lat_angle = ((row_ids + 0.5) * (math.pi / total_rows))[:, None] * frequency[None, :]
    lon_angle = (col_ids * (2.0 * math.pi / total_cols))[:, None] * frequency[None, :]
    lat_cos = jnp.cos(lat_angle)[:, None, None, :]
    lat_sin = jnp.sin(lat_angle)[:, None, None, :]
    lon_cos = jnp.cos(lon_angle)[None, :, None, :]
    lon_sin = jnp.sin(lon_angle)[None, :, None, :]
    quarters = values.astype(jnp.float32).reshape(band_rows, sector_cols, head_count, 4, quarter)
    lat_one = quarters[:, :, :, 0, :]
    lat_two = quarters[:, :, :, 1, :]
    lon_one = quarters[:, :, :, 2, :]
    lon_two = quarters[:, :, :, 3, :]
    turned = jnp.stack(
        [
            lat_one * lat_cos - lat_two * lat_sin,
            lat_one * lat_sin + lat_two * lat_cos,
            lon_one * lon_cos - lon_two * lon_sin,
            lon_one * lon_sin + lon_two * lon_cos,
        ],
        axis=3,
    )
    return turned.reshape(band_rows, sector_cols, feature_width).astype(jnp.bfloat16)


def widen_rows(stacked, radius):
    padded = extended_2(stacked, (("lat", 1),), radius, False)
    return padded[:, : padded.shape[1] - 1]


def widen_cols(stacked, radius):
    padded = extended_2(stacked, (("lon", 2),), radius, True)
    return padded[:, :, : padded.shape[2] - 1]


def shards_halo(query_tok, key_tok, value_tok, query_tan, key_tan, value_tan):
    band_rows, sector_cols, feature_width = query_tok.shape
    radius = WIN // 2
    window_span = 2 * radius
    score_scale = 1.0 / math.sqrt(HD)
    total_rows = band_rows * lax.axis_size("lat")
    total_cols = sector_cols * lax.axis_size("lon")
    row_first = lax.axis_index("lat") * band_rows
    col_first = lax.axis_index("lon") * sector_cols
    rot_query = rotate_rays(query_tok, row_first, col_first, total_rows, total_cols)
    rot_qtan = rotate_rays(query_tan, row_first, col_first, total_rows, total_cols)
    rot_key = rotate_rays(key_tok, row_first, col_first, total_rows, total_cols)
    rot_ktan = rotate_rays(key_tan, row_first, col_first, total_rows, total_cols)
    stacked = jnp.stack([rot_key, rot_ktan, value_tok, value_tan])
    extended = widen_rows(widen_cols(stacked, radius), radius)
    ext_rows = band_rows + window_span - 1
    ext_cols = sector_cols + window_span - 1
    key_count = ext_rows * ext_cols
    query_count = band_rows * sector_cols
    keys_flat = extended.reshape(4, key_count, feature_width)
    query_flat = rot_query.reshape(query_count, feature_width)
    qtan_flat = rot_qtan.reshape(query_count, feature_width)
    key_ids = jnp.arange(key_count, dtype=jnp.int32)
    query_ids = jnp.arange(query_count, dtype=jnp.int32)
    row_gap = (key_ids // ext_cols)[None, :] - (query_ids // sector_cols)[:, None]
    col_gap = (key_ids % ext_cols)[None, :] - (query_ids % sector_cols)[:, None]
    key_rows = row_first - radius + key_ids // ext_cols
    allowed = (
        (row_gap >= 0)
        & (row_gap < window_span)
        & (col_gap >= 0)
        & (col_gap < window_span)
        & ((key_rows >= 0) & (key_rows < total_rows))[None, :]
    )
    head_count = feature_width // HD
    group_size = math.gcd(head_count, 4)
    out_groups = []
    tan_groups = []
    for group_index in range(head_count // group_size):
        low_col = group_index * group_size * HD
        high_col = low_col + group_size * HD
        q_part = query_flat[:, low_col:high_col].reshape(query_count, group_size, HD)
        qt_part = qtan_flat[:, low_col:high_col].reshape(query_count, group_size, HD)
        k_part = keys_flat[0][:, low_col:high_col].reshape(key_count, group_size, HD)
        kt_part = keys_flat[1][:, low_col:high_col].reshape(key_count, group_size, HD)
        v_part = keys_flat[2][:, low_col:high_col].reshape(key_count, group_size, HD)
        vt_part = keys_flat[3][:, low_col:high_col].reshape(key_count, group_size, HD)
        scores = (
            jnp.einsum("qhd,khd->hqk", q_part, k_part, preferred_element_type=jnp.float32)
            * score_scale
        )
        scores = jnp.where(allowed[None], scores, -1e30)
        row_top = jnp.max(scores, axis=-1, keepdims=True)
        exp_scores = jnp.exp(scores - row_top)
        attention = exp_scores / jnp.sum(exp_scores, axis=-1, keepdims=True)
        slopes = (
            jnp.einsum("qhd,khd->hqk", qt_part, k_part, preferred_element_type=jnp.float32)
            + jnp.einsum("qhd,khd->hqk", q_part, kt_part, preferred_element_type=jnp.float32)
        ) * score_scale
        mean_slope = jnp.sum(attention * slopes, axis=-1, keepdims=True)
        weight_b = (attention * (slopes - mean_slope)).astype(jnp.bfloat16)
        prob_b = attention.astype(jnp.bfloat16)
        group_out = jnp.einsum("hqk,khd->qhd", prob_b, v_part, preferred_element_type=jnp.float32)
        group_tan = jnp.einsum(
            "hqk,khd->qhd", weight_b, v_part, preferred_element_type=jnp.float32
        ) + jnp.einsum("hqk,khd->qhd", prob_b, vt_part, preferred_element_type=jnp.float32)
        out_groups.append(group_out.reshape(query_count, group_size * HD))
        tan_groups.append(group_tan.reshape(query_count, group_size * HD))
    attended = jnp.concatenate(out_groups, axis=1).astype(jnp.bfloat16)
    attended_tan = jnp.concatenate(tan_groups, axis=1).astype(jnp.bfloat16)
    return (
        attended.reshape(band_rows, sector_cols, feature_width),
        attended_tan.reshape(band_rows, sector_cols, feature_width),
    )


BF = jnp.bfloat16
F32 = jnp.float32
MESH = pl.DeviceIdType.MESH


def ray_tables(total_rows, total_cols):
    quarter = HD // 4
    freq = (np.arange(quarter) + 1).astype(np.float32)
    rows = np.arange(total_rows).astype(np.float32)
    cols = np.arange(total_cols).astype(np.float32)
    lat = ((rows + np.float32(0.5)) * np.float32(math.pi / total_rows))[:, None] * freq[None, :]
    lon = (cols * np.float32(2.0 * math.pi / total_cols))[:, None] * freq[None, :]

    def table(fn, angle, first):
        part = fn(angle.astype(np.float64)).astype(np.float32)
        none = np.zeros_like(part)
        return np.concatenate([part, part, none, none] if first else [none, none, part, part], axis=1)

    row_tab = np.stack([table(np.cos, lat, True), table(np.sin, lat, True)])
    col_tab = np.stack([table(np.cos, lon, False), table(np.sin, lon, False)])
    return row_tab, col_tab


def kernel(
    n, n_lon, hp, band,
    q_ref, k_ref, v_ref, qt_ref, kt_ref, vt_ref, row_hbm, col_hbm,
    both_ref,
    raw_kv, raw_q, kvb, hs, outs, turn, bias, row_tab, col_tab,
    in_send, in_recv, in_loc, h_send, h_recv, o_send, o_recv, o_loc, t_loc,
):
    me = lax.axis_index("lat")
    lon = lax.axis_index("lon")
    left = lax.rem(lon + n_lon - 1, n_lon)
    right = lax.rem(lon + 1, n_lon)
    cols = 16
    total = n * band
    pairs = total // 2

    here = pl.ds(pl.multiple_of(lon * cols, cols), cols)
    row_copy = pltpu.make_async_copy(row_hbm, row_tab, t_loc.at[0])
    col_copy = pltpu.make_async_copy(col_hbm.at[:, here], col_tab, t_loc.at[1])
    row_copy.start()
    col_copy.start()

    barrier = pltpu.get_barrier_semaphore()
    for d in range(1, n):
        pl.semaphore_signal(barrier, inc=1, device_id=(lax.rem(me + d, n), lon), device_id_type=MESH)
    for side in (left, right):
        pl.semaphore_signal(barrier, inc=1, device_id=(me, side), device_id_type=MESH)
    pl.semaphore_wait(barrier, n + 1)

    kv_refs = (k_ref, kt_ref, v_ref, vt_ref)
    q_refs = (q_ref, qt_ref)

    def lanes(owner, j):
        return pl.ds(pl.multiple_of((owner * hp + j) * HD, HD), HD)

    def in_copy(a, j, d):
        peer = lax.rem(me + d, n)
        ref = kv_refs[a] if a < 4 else q_refs[a - 4]
        dst = raw_kv.at[j, a] if a < 4 else raw_q.at[j, a - 4]
        return pltpu.make_async_remote_copy(
            src_ref=ref.at[:, :, lanes(peer, j)],
            dst_ref=dst.at[pl.ds(me * band, band)],
            send_sem=in_send.at[j, a, d - 1],
            recv_sem=in_recv.at[j, a, d - 1],
            device_id=(peer, lon),
            device_id_type=MESH,
        )

    def own_copy(a, j):
        ref = kv_refs[a] if a < 4 else q_refs[a - 4]
        dst = raw_kv.at[j, a] if a < 4 else raw_q.at[j, a - 4]
        return pltpu.make_async_copy(
            ref.at[:, :, lanes(me, j)], dst.at[pl.ds(me * band, band)], in_loc.at[j, a]
        )

    def halo_copy(side, j):
        return pltpu.make_async_remote_copy(
            src_ref=hs.at[j, side],
            dst_ref=kvb.at[j, :, :, 3 - side],
            send_sem=h_send.at[j, side],
            recv_sem=h_recv.at[j, side],
            device_id=(me, right if side else left),
            device_id_type=MESH,
        )

    def out_copy(o, j, d):
        peer = lax.rem(me + d, n)
        return pltpu.make_async_remote_copy(
            src_ref=outs.at[j, o, pl.ds(peer * band, band)],
            dst_ref=both_ref.at[o, :, :, lanes(me, j)],
            send_sem=o_send.at[j, o, d - 1],
            recv_sem=o_recv.at[j, o, d - 1],
            device_id=(peer, lon),
            device_id_type=MESH,
        )

    def own_out(o, j):
        return pltpu.make_async_copy(
            outs.at[j, o, pl.ds(me * band, band)],
            both_ref.at[o, :, :, lanes(me, j)],
            o_loc.at[j, o],
        )

    @pl.loop(0, hp)
    def _(j):
        for a in range(4):
            for d in range(1, n):
                in_copy(a, j, d).start()
        for a in range(4):
            own_copy(a, j).start()

    @pl.loop(0, hp)
    def _(j):
        for a in range(4, 6):
            for d in range(1, n):
                in_copy(a, j, d).start()
        for a in range(4, 6):
            own_copy(a, j).start()

    row_copy.wait()
    col_copy.wait()
    for t in range(2):
        whole = row_tab[t][:, None, :] + col_tab[t][None, :, :]
        turn[t] = whole.reshape(total * cols, HD)
    shape = (band * cols, (band + WIN) * 2 * cols)
    query = lax.broadcasted_iota(jnp.int32, shape, 0)
    key = lax.broadcasted_iota(jnp.int32, shape, 1)
    part = (key % 64) // 16
    spot = key % 16
    own = part < 2
    key_row = (key // 64) * 2 + jnp.where(own, part, spot // 8)
    key_col = jnp.where(own, spot, jnp.where(part == 2, spot % 8 - 8, spot % 8 + 16))
    row_gap = key_row - query // 16
    col_gap = key_col - query % 16 + WIN // 2
    allowed = (row_gap >= 0) & (row_gap < WIN) & (col_gap >= 0) & (col_gap < WIN)
    bias[...] = jnp.where(allowed, 0.0, -1e30)
    src = lax.broadcasted_iota(jnp.int32, (HD, HD), 0)
    dst = lax.broadcasted_iota(jnp.int32, (HD, HD), 1)
    low = (dst % 64) < 32
    swap = (
        jnp.where(low & (src == dst + 32), -1.0, 0.0)
        + jnp.where(jnp.logical_not(low) & (src == dst - 32), 1.0, 0.0)
    ).astype(BF)

    def turned(x):
        flat = x.reshape(total * cols, HD)
        other = jnp.dot(flat, swap, preferred_element_type=F32)
        return flat.astype(F32) * turn[0] + other * turn[1]

    @pl.loop(0, hp)
    def _(j):
        for a in range(4):
            own_copy(a, j).wait()
            for d in range(1, n):
                in_copy(a, j, d).wait_recv()
            x = raw_kv[j, a]
            y = turned(x) if a < 2 else x.reshape(total * cols, HD).astype(F32)
            kvb[j, a, :, 0:2] = y.reshape(pairs, 2, cols, HD).astype(BF)
            halves = y.reshape(total, 2, cols // 2, HD)
            for side in range(2):
                hs[j, side, a] = halves[:, side].reshape(pairs, cols, HD).astype(BF)
        for side in range(2):
            halo_copy(side, j).start()

    scale2 = math.log2(math.e) / math.sqrt(HD)
    scale = 1.0 / math.sqrt(HD)

    @pl.loop(0, hp)
    def _(j):
        for a in range(4, 6):
            own_copy(a, j).wait()
            for d in range(1, n):
                in_copy(a, j, d).wait_recv()
            raw_q[j, a - 4] = turned(raw_q[j, a - 4]).astype(BF).reshape(total, cols, HD)
        for side in range(2):
            halo_copy(side, j).wait_recv()
        nq = band * cols
        for b in range(n):
            first = max(0, b * band - WIN // 2)
            last = min(total, (b + 1) * band + WIN // 2)
            skip = (first - (b * band - WIN // 2)) // 2 * 64
            p0, p1 = first // 2, last // 2
            nk = (p1 - p0) * 64
            keys = kvb[j, 0, p0:p1].reshape(nk, HD)
            ktan = kvb[j, 1, p0:p1].reshape(nk, HD)
            val = kvb[j, 2, p0:p1].reshape(nk, HD)
            vtan = kvb[j, 3, p0:p1].reshape(nk, HD)
            rows = slice(b * band, (b + 1) * band)
            q = raw_q[j, 0, rows].reshape(nq, HD)
            qt = raw_q[j, 1, rows].reshape(nq, HD)
            nt = (((1,), (1,)), ((), ()))
            score = lax.dot_general(q, keys, nt, preferred_element_type=F32)
            score = score * scale2 + bias[:, skip:skip + nk]
            top = jnp.max(score, axis=-1, keepdims=True)
            e = jnp.exp2(score - top)
            inv = 1.0 / jnp.sum(e, axis=-1, keepdims=True)
            slope = lax.dot_general(
                jnp.concatenate([qt, q], axis=1),
                jnp.concatenate([keys, ktan], axis=1),
                nt,
                preferred_element_type=F32,
            )
            mean = jnp.sum(e * slope, axis=-1, keepdims=True) * inv
            prob = e * inv
            prob_b = prob.astype(BF)
            weight_b = (prob * ((slope - mean) * scale)).astype(BF)
            both = jnp.dot(
                prob_b, jnp.concatenate([val, vtan], axis=1), preferred_element_type=F32
            )
            tan = both[:, HD:] + jnp.dot(weight_b, val, preferred_element_type=F32)
            outs[j, 0, rows] = both[:, :HD].astype(BF).reshape(band, cols, HD)
            outs[j, 1, rows] = tan.astype(BF).reshape(band, cols, HD)

            @pl.when(me == b)
            def _():
                for o in range(2):
                    own_out(o, j).start()

            @pl.when(me != b)
            def _():
                for o in range(2):
                    out_copy(o, j, lax.rem(b - me + n, n)).start()
    @pl.loop(0, hp)
    def _(j):
        for a in range(6):
            for d in range(1, n):
                in_copy(a, j, d).wait_send()
        for side in range(2):
            halo_copy(side, j).wait_send()
        for o in range(2):
            own_out(o, j).wait()
            for d in range(1, n):
                out_copy(o, j, d).wait()


def shards(mesh_shape, *args):
    band, cols, width = args[0].shape
    n, n_lon = mesh_shape["lat"], mesh_shape["lon"]
    heads = width // HD
    fits = heads % n == 0 and n > 1 and n_lon > 2 and cols == WIN and band == WIN // 2
    if not fits:
        return shards_halo(*args)
    hp = heads // n
    total = band * n
    row_tab, col_tab = ray_tables(total, cols * n_lon)
    hbm = pl.BlockSpec(memory_space=pltpu.HBM)
    anywhere = pl.BlockSpec(memory_space=pl.ANY)
    q, k, v, qt, kt, vt = args
    dma = pltpu.SemaphoreType.DMA
    nq = band * cols
    nk = (band + WIN) * 2 * cols
    both = (
        pl.pallas_call(
            functools.partial(kernel, n, n_lon, hp, band),
            out_shape=pltpu.VMEM((2, band, cols, width), BF),
            in_specs=[hbm] * 8,
            out_specs=anywhere,
            scratch_shapes=[
                pltpu.VMEM((hp, 4, total, cols, HD), BF),
                pltpu.VMEM((hp, 2, total, cols, HD), BF),
                pltpu.VMEM((hp, 4, total // 2, 4, cols, HD), BF),
                pltpu.VMEM((hp, 2, 4, total // 2, cols, HD), BF),
                pltpu.VMEM((hp, 2, total, cols, HD), BF),
                pltpu.VMEM((2, total * cols, HD), F32),
                pltpu.VMEM((nq, nk), F32),
                pltpu.VMEM((2, total, HD), F32),
                pltpu.VMEM((2, cols, HD), F32),
                dma((hp, 6, n - 1)),
                dma((hp, 6, n - 1)),
                dma((hp, 6)),
                dma((hp, 2)),
                dma((hp, 2)),
                dma((hp, 2, n - 1)),
                dma((hp, 2, n - 1)),
                dma((hp, 2)),
                dma((2,)),
            ],
            compiler_params=pltpu.CompilerParams(
                collective_id=0, has_side_effects=True, vmem_limit_bytes=60 * 1024 * 1024
            ),
            name="panorama",
        )(q, k, v, qt, kt, vt, jnp.asarray(row_tab), jnp.asarray(col_tab))
    )
    return both[0], both[1]


def solution(mesh):
    placed = (
        P("lat", "lon", None),
        P("lat", "lon", None),
        P("lat", "lon", None),
        P("lat", "lon", None),
        P("lat", "lon", None),
        P("lat", "lon", None),
    )
    return jax.shard_map(
        functools.partial(shards, dict(mesh.shape)),
        mesh=mesh,
        in_specs=placed,
        out_specs=(P("lat", "lon", None), P("lat", "lon", None)),
        check_vma=False,
    )
```

profile of v0, /device:TPU:0, one launch (start us, length us, event | category | flops | bytes accessed | tf_op | source)
XLA Modules:
  0.0 42.9 jit_solution(13310262338837440212)
XLA Ops:
  0.6 41.4 %panorama.1 = bf16[2,8,16,1536]{3,2,1,0:T(8,128)(2,1)S(1)} custom-call(bf16[8,16,1536]{2,1,0:T(8,128)(2,1)} %q_ref.1, bf16[8,16,1536]{2,1,0:T(8,128)(2,1)} %k_ref.1, bf16[8,16,1536]{2,1,0:T(8,128)(2,1)} %v_ref.1, bf16[8,16,1536]{2,1,0:T(8,128)(2,1)} %qt_ref.1, bf16[8,16,1536]{2,1,0:T(8,128)(2,1)} %kt_ref.1, bf16[8,16,1536]{2,1,0:T(8,128)(2,1)} %vt_ref.1, ...), custom_call_target="tpu_custom_call" | custom-call | tf_op jit(solution)/shard_map/panorama/pallas_call | solution.py:399
  42.0 0.9 %slice_bitcast_fusion = (bf16[8,16,1536]{2,1,0:T(8,128)(2,1)}, bf16[8,16,1536]{2,1,0:T(8,128)(2,1)}) fusion(bf16[2,8,16,1536]{3,2,1,0:T(8,128)(2,1)S(1)} %panorama.1), kind=kLoop, calls=%fused_computation | loop fusion | bytes 1572864 | tf_op jit(solution)/shard_map/squeeze | solution.py:430
where the time goes:
time: 43.1 us; the launch traced here: 42.9 us
  Pallas kernels  41.4 us (96%)
  local copies, waits for them, and re-layouts  0.93 us (2%)
  between operations  0.64 us (1%)
    pallas_call x1, Pallas kernels, shards(): pl.pallas_call(functools.partial(kernel, n, n_lon, hp, band), out_shape=p...  41.4 us
    squeeze x1, local copies, waits for them, and re-layouts, shards(): return (both[0], both[1])  0.93 us

commit v1 on v0

--- a/solution.py
+++ b/solution.py
@@ -170,7 +170,7 @@
     q_ref, k_ref, v_ref, qt_ref, kt_ref, vt_ref, row_hbm, col_hbm,
     both_ref,
     raw_kv, raw_q, kvb, hs, outs, turn, bias, row_tab, col_tab,
-    in_send, in_recv, in_loc, h_send, h_recv, o_send, o_recv, o_loc, t_loc,
+    kv_send, kv_recv, q_send, q_recv, in_loc, q_loc, h_send, h_recv, o_send, o_recv, o_loc, t_loc, greet,
 ):
     me = lax.axis_index("lat")
     lon = lax.axis_index("lon")
@@ -180,88 +180,136 @@
     total = n * band
     pairs = total // 2
 
+    barrier = pltpu.get_barrier_semaphore()
+    for d in range(1, n):
+        pl.semaphore_signal(barrier, inc=1, device_id=(lax.rem(me + d, n), lon), device_id_type=MESH)
+
+    def tell(sem, side):
+        pl.semaphore_signal(sem, inc=1, device_id=(me, side), device_id_type=MESH)
+
+    first, last = lon == 0, lon == n_lon - 1
+    odd = lax.rem(lon, 2) == 1
+    middle_odd = jnp.logical_and(odd, jnp.logical_not(last))
+    middle_even = jnp.logical_and(jnp.logical_not(odd), jnp.logical_not(first))
+
+    @pl.when(middle_odd)
+    def _():
+        tell(barrier, left)
+        tell(barrier, right)
+        pl.semaphore_wait(barrier, n - 1)
+
+    @pl.when(middle_even)
+    def _():
+        pl.semaphore_wait(barrier, n + 1)
+        tell(greet, left)
+        tell(greet, right)
+
+    @pl.when(first)
+    def _():
+        tell(barrier, left)
+        pl.semaphore_wait(barrier, n)
+        tell(greet, right)
+
+    @pl.when(last)
+    def _():
+        tell(barrier, left)
+        pl.semaphore_wait(barrier, n)
+        tell(greet, right)
+
+    kv_refs = (k_ref, kt_ref, v_ref, vt_ref)
+    q_refs = (q_ref, qt_ref)
+    parts = ((0, 1), (1, hp - 1)) if hp > 1 else ((0, 1),)
+
+    def lanes(owner, j, count):
+        return pl.ds(pl.multiple_of((owner * hp + j) * HD, HD), count * HD)
+
+    def kv_copy(a, p, d):
+        peer = lax.rem(me + d, n)
+        j, count = parts[p]
+        return pltpu.make_async_remote_copy(
+            src_ref=kv_refs[a].at[:, :, lanes(peer, j, count)],
+            dst_ref=raw_kv.at[a, pl.ds(me * band, band), :, j * HD:(j + count) * HD],
+            send_sem=kv_send.at[a, p, d - 1],
+            recv_sem=kv_recv.at[a, p, d - 1],
+            device_id=(peer, lon),
+            device_id_type=MESH,
+        )
+
+    def q_copy(a, j, d):
+        peer = lax.rem(me + d, n)
+        return pltpu.make_async_remote_copy(
+            src_ref=q_refs[a].at[:, :, lanes(peer, j, 1)],
+            dst_ref=raw_q.at[j, a, pl.ds(me * band, band)],
+            send_sem=q_send.at[j, a, d - 1],
+            recv_sem=q_recv.at[j, a, d - 1],
+            device_id=(peer, lon),
+            device_id_type=MESH,
+        )
+
+    def own_q(a, j):
+        return pltpu.make_async_copy(
+            q_refs[a].at[:, :, lanes(me, j, 1)],
+            raw_q.at[j, a, pl.ds(me * band, band)],
+            q_loc.at[j, a],
+        )
+
+    def own_copy(a, p):
+        j, count = parts[p]
+        return pltpu.make_async_copy(
+            kv_refs[a].at[:, :, lanes(me, j, count)],
+            raw_kv.at[a, pl.ds(me * band, band), :, j * HD:(j + count) * HD],
+            in_loc.at[a, p],
+        )
+
+    halos = [(0, slice(0, 4))] + [(p, slice(a, a + 1)) for p in range(1, len(parts)) for a in range(4)]
+
+    def halo_copy(side, h):
+        p, arrays = halos[h]
+        j, count = parts[p]
+        return pltpu.make_async_remote_copy(
+            src_ref=hs.at[side, arrays, j:j + count],
+            dst_ref=kvb.at[arrays, j:j + count, :, 3 - side],
+            send_sem=h_send.at[h, side],
+            recv_sem=h_recv.at[h, side],
+            device_id=(me, right if side else left),
+            device_id_type=MESH,
+        )
+
+    def out_copy(j, d):
+        peer = lax.rem(me + d, n)
+        return pltpu.make_async_remote_copy(
+            src_ref=outs.at[j, :, pl.ds(peer * band, band)],
+            dst_ref=both_ref.at[:, :, :, lanes(me, j, 1)],
+            send_sem=o_send.at[j, d - 1],
+            recv_sem=o_recv.at[j, d - 1],
+            device_id=(peer, lon),
+            device_id_type=MESH,
+        )
+
+    def own_out(j):
+        return pltpu.make_async_copy(
+            outs.at[j, :, pl.ds(me * band, band)],
+            both_ref.at[:, :, :, lanes(me, j, 1)],
+            o_loc.at[j],
+        )
+
     here = pl.ds(pl.multiple_of(lon * cols, cols), cols)
     row_copy = pltpu.make_async_copy(row_hbm, row_tab, t_loc.at[0])
     col_copy = pltpu.make_async_copy(col_hbm.at[:, here], col_tab, t_loc.at[1])
     row_copy.start()
     col_copy.start()
-
-    barrier = pltpu.get_barrier_semaphore()
-    for d in range(1, n):
-        pl.semaphore_signal(barrier, inc=1, device_id=(lax.rem(me + d, n), lon), device_id_type=MESH)
-    for side in (left, right):
-        pl.semaphore_signal(barrier, inc=1, device_id=(me, side), device_id_type=MESH)
-    pl.semaphore_wait(barrier, n + 1)
-
-    kv_refs = (k_ref, kt_ref, v_ref, vt_ref)
-    q_refs = (q_ref, qt_ref)
-
-    def lanes(owner, j):
-        return pl.ds(pl.multiple_of((owner * hp + j) * HD, HD), HD)
-
-    def in_copy(a, j, d):
-        peer = lax.rem(me + d, n)
-        ref = kv_refs[a] if a < 4 else q_refs[a - 4]
-        dst = raw_kv.at[j, a] if a < 4 else raw_q.at[j, a - 4]
-        return pltpu.make_async_remote_copy(
-            src_ref=ref.at[:, :, lanes(peer, j)],
-            dst_ref=dst.at[pl.ds(me * band, band)],
-            send_sem=in_send.at[j, a, d - 1],
-            recv_sem=in_recv.at[j, a, d - 1],
-            device_id=(peer, lon),
-            device_id_type=MESH,
-        )
-
-    def own_copy(a, j):
-        ref = kv_refs[a] if a < 4 else q_refs[a - 4]
-        dst = raw_kv.at[j, a] if a < 4 else raw_q.at[j, a - 4]
-        return pltpu.make_async_copy(
-            ref.at[:, :, lanes(me, j)], dst.at[pl.ds(me * band, band)], in_loc.at[j, a]
-        )
-
-    def halo_copy(side, j):
-        return pltpu.make_async_remote_copy(
-            src_ref=hs.at[j, side],
-            dst_ref=kvb.at[j, :, :, 3 - side],
-            send_sem=h_send.at[j, side],
-            recv_sem=h_recv.at[j, side],
-            device_id=(me, right if side else left),
-            device_id_type=MESH,
-        )
-
-    def out_copy(o, j, d):
-        peer = lax.rem(me + d, n)
-        return pltpu.make_async_remote_copy(
-            src_ref=outs.at[j, o, pl.ds(peer * band, band)],
-            dst_ref=both_ref.at[o, :, :, lanes(me, j)],
-            send_sem=o_send.at[j, o, d - 1],
-            recv_sem=o_recv.at[j, o, d - 1],
-            device_id=(peer, lon),
-            device_id_type=MESH,
-        )
-
-    def own_out(o, j):
-        return pltpu.make_async_copy(
-            outs.at[j, o, pl.ds(me * band, band)],
-            both_ref.at[o, :, :, lanes(me, j)],
-            o_loc.at[j, o],
-        )
-
-    @pl.loop(0, hp)
-    def _(j):
+    for p in range(len(parts)):
         for a in range(4):
             for d in range(1, n):
-                in_copy(a, j, d).start()
+                kv_copy(a, p, d).start()
         for a in range(4):
-            own_copy(a, j).start()
-
-    @pl.loop(0, hp)
-    def _(j):
-        for a in range(4, 6):
+            own_copy(a, p).start()
+    for j in range(hp):
+        for a in range(2):
             for d in range(1, n):
-                in_copy(a, j, d).start()
-        for a in range(4, 6):
-            own_copy(a, j).start()
+                q_copy(a, j, d).start()
+        for a in range(2):
+            own_q(a, j).start()
 
     row_copy.wait()
     col_copy.wait()
@@ -293,33 +341,54 @@
         other = jnp.dot(flat, swap, preferred_element_type=F32)
         return flat.astype(F32) * turn[0] + other * turn[1]
 
+    def stage(a, j):
+        x = raw_kv[a, :, :, pl.ds(pl.multiple_of(j * HD, HD), HD)]
+        y = turned(x) if a < 2 else x.reshape(total * cols, HD).astype(F32)
+        kvb[a, j, :, 0:2] = y.reshape(pairs, 2, cols, HD).astype(BF)
+        halves = y.reshape(total, 2, cols // 2, HD)
+        for side in range(2):
+            hs[side, a, j] = halves[:, side].reshape(pairs, cols, HD).astype(BF)
+
+    @pl.when(middle_odd)
+    def _():
+        pl.semaphore_wait(greet, 2)
+
+    @pl.when(jnp.logical_or(first, last))
+    def _():
+        pl.semaphore_wait(greet, 1)
+
+    for p in range(len(parts)):
+        for a in range(4):
+            own_copy(a, p).wait()
+            for d in range(1, n):
+                kv_copy(a, p, d).wait_recv()
+            if parts[p][1] == 1:
+                stage(a, parts[p][0])
+            else:
+                pl.loop(parts[p][0], sum(parts[p]))(functools.partial(stage, a))
+            for h in range(len(halos)):
+                if halos[h][0] == p and halos[h][1].stop == a + 1:
+                    for side in range(2):
+                        halo_copy(side, h).start()
+
+    scale2 = math.log2(math.e) / math.sqrt(HD)
+    scale = 1.0 / math.sqrt(HD)
+
     @pl.loop(0, hp)
     def _(j):
-        for a in range(4):
-            own_copy(a, j).wait()
+        for p in range(len(parts)):
+            @pl.when(j == parts[p][0])
+            def _():
+                for h in range(len(halos)):
+                    if halos[h][0] == p:
+                        for side in range(2):
+                            halo_copy(side, h).wait_recv()
+
+        for a in range(2):
+            own_q(a, j).wait()
             for d in range(1, n):
-                in_copy(a, j, d).wait_recv()
-            x = raw_kv[j, a]
-            y = turned(x) if a < 2 else x.reshape(total * cols, HD).astype(F32)
-            kvb[j, a, :, 0:2] = y.reshape(pairs, 2, cols, HD).astype(BF)
-            halves = y.reshape(total, 2, cols // 2, HD)
-            for side in range(2):
-                hs[j, side, a] = halves[:, side].reshape(pairs, cols, HD).astype(BF)
-        for side in range(2):
-            halo_copy(side, j).start()
-
-    scale2 = math.log2(math.e) / math.sqrt(HD)
-    scale = 1.0 / math.sqrt(HD)
-
-    @pl.loop(0, hp)
-    def _(j):
-        for a in range(4, 6):
-            own_copy(a, j).wait()
-            for d in range(1, n):
-                in_copy(a, j, d).wait_recv()
-            raw_q[j, a - 4] = turned(raw_q[j, a - 4]).astype(BF).reshape(total, cols, HD)
-        for side in range(2):
-            halo_copy(side, j).wait_recv()
+                q_copy(a, j, d).wait_recv()
+            raw_q[j, a] = turned(raw_q[j, a]).astype(BF).reshape(total, cols, HD)
         nq = band * cols
         for b in range(n):
             first = max(0, b * band - WIN // 2)
@@ -327,10 +396,10 @@
             skip = (first - (b * band - WIN // 2)) // 2 * 64
             p0, p1 = first // 2, last // 2
             nk = (p1 - p0) * 64
-            keys = kvb[j, 0, p0:p1].reshape(nk, HD)
-            ktan = kvb[j, 1, p0:p1].reshape(nk, HD)
-            val = kvb[j, 2, p0:p1].reshape(nk, HD)
-            vtan = kvb[j, 3, p0:p1].reshape(nk, HD)
+            keys = kvb[0, j, p0:p1].reshape(nk, HD)
+            ktan = kvb[1, j, p0:p1].reshape(nk, HD)
+            val = kvb[2, j, p0:p1].reshape(nk, HD)
+            vtan = kvb[3, j, p0:p1].reshape(nk, HD)
             rows = slice(b * band, (b + 1) * band)
             q = raw_q[j, 0, rows].reshape(nq, HD)
             qt = raw_q[j, 1, rows].reshape(nq, HD)
@@ -359,31 +428,35 @@
 
             @pl.when(me == b)
             def _():
-                for o in range(2):
-                    own_out(o, j).start()
+                own_out(j).start()
 
             @pl.when(me != b)
             def _():
-                for o in range(2):
-                    out_copy(o, j, lax.rem(b - me + n, n)).start()
-    @pl.loop(0, hp)
-    def _(j):
-        for a in range(6):
-            for d in range(1, n):
-                in_copy(a, j, d).wait_send()
+                out_copy(j, lax.rem(b - me + n, n)).start()
+
+    for p in range(len(parts)):
+        for d in range(1, n):
+            for a in range(4):
+                kv_copy(a, p, d).wait_send()
+    for h in range(len(halos)):
         for side in range(2):
-            halo_copy(side, j).wait_send()
-        for o in range(2):
-            own_out(o, j).wait()
-            for d in range(1, n):
-                out_copy(o, j, d).wait()
+            halo_copy(side, h).wait_send()
+    for j in range(hp):
+        own_out(j).wait()
+        for d in range(1, n):
+            for a in range(2):
+                q_copy(a, j, d).wait_send()
+            out_copy(j, d).wait()
 
 
 def shards(mesh_shape, *args):
     band, cols, width = args[0].shape
     n, n_lon = mesh_shape["lat"], mesh_shape["lon"]
     heads = width // HD
-    fits = heads % n == 0 and n > 1 and n_lon > 2 and cols == WIN and band == WIN // 2
+    fits = (
+        heads % n == 0 and n > 1 and n_lon > 2 and n_lon % 2 == 0
+        and cols == WIN and band == WIN // 2
+    )
     if not fits:
         return shards_halo(*args)
     hp = heads // n
@@ -395,38 +468,40 @@
     dma = pltpu.SemaphoreType.DMA
     nq = band * cols
     nk = (band + WIN) * 2 * cols
-    both = (
-        pl.pallas_call(
-            functools.partial(kernel, n, n_lon, hp, band),
-            out_shape=pltpu.VMEM((2, band, cols, width), BF),
-            in_specs=[hbm] * 8,
-            out_specs=anywhere,
-            scratch_shapes=[
-                pltpu.VMEM((hp, 4, total, cols, HD), BF),
-                pltpu.VMEM((hp, 2, total, cols, HD), BF),
-                pltpu.VMEM((hp, 4, total // 2, 4, cols, HD), BF),
-                pltpu.VMEM((hp, 2, 4, total // 2, cols, HD), BF),
-                pltpu.VMEM((hp, 2, total, cols, HD), BF),
-                pltpu.VMEM((2, total * cols, HD), F32),
-                pltpu.VMEM((nq, nk), F32),
-                pltpu.VMEM((2, total, HD), F32),
-                pltpu.VMEM((2, cols, HD), F32),
-                dma((hp, 6, n - 1)),
-                dma((hp, 6, n - 1)),
-                dma((hp, 6)),
-                dma((hp, 2)),
-                dma((hp, 2)),
-                dma((hp, 2, n - 1)),
-                dma((hp, 2, n - 1)),
-                dma((hp, 2)),
-                dma((2,)),
-            ],
-            compiler_params=pltpu.CompilerParams(
-                collective_id=0, has_side_effects=True, vmem_limit_bytes=60 * 1024 * 1024
-            ),
-            name="panorama",
-        )(q, k, v, qt, kt, vt, jnp.asarray(row_tab), jnp.asarray(col_tab))
-    )
+    both = pl.pallas_call(
+        functools.partial(kernel, n, n_lon, hp, band),
+        out_shape=pltpu.VMEM((2, band, cols, width), BF),
+        in_specs=[hbm] * 8,
+        out_specs=anywhere,
+        scratch_shapes=[
+            pltpu.VMEM((4, total, cols, hp * HD), BF),
+            pltpu.VMEM((hp, 2, total, cols, HD), BF),
+            pltpu.VMEM((4, hp, total // 2, 4, cols, HD), BF),
+            pltpu.VMEM((2, 4, hp, total // 2, cols, HD), BF),
+            pltpu.VMEM((hp, 2, total, cols, HD), BF),
+            pltpu.VMEM((2, total * cols, HD), F32),
+            pltpu.VMEM((nq, nk), F32),
+            pltpu.VMEM((2, total, HD), F32),
+            pltpu.VMEM((2, cols, HD), F32),
+            dma((4, 2, n - 1)),
+            dma((4, 2, n - 1)),
+            dma((hp, 2, n - 1)),
+            dma((hp, 2, n - 1)),
+            dma((4, 2)),
+            dma((hp, 2)),
+            dma((5, 2)),
+            dma((5, 2)),
+            dma((hp, n - 1)),
+            dma((hp, n - 1)),
+            dma((hp,)),
+            dma((2,)),
+            pltpu.SemaphoreType.REGULAR,
+        ],
+        compiler_params=pltpu.CompilerParams(
+            collective_id=0, has_side_effects=True, vmem_limit_bytes=60 * 1024 * 1024
+        ),
+        name="panorama",
+    )(q, k, v, qt, kt, vt, jnp.asarray(row_tab), jnp.asarray(col_tab))
     return both[0], both[1]
 
 

time: 43.1 us -> 41.5 us (0.963); the launches traced: 42.9 us -> 40.7 us
  Pallas kernels: 41.4 us -> 39.1 us
    pallas_call x1, Pallas kernels: 41.4 us -> 39.1 us  [shards(): pl.pallas_call(functools.partial(kernel, n, n_lon, hp, band), out_shape=p...]
where the time goes in v1:
time: 41.5 us; the launch traced here: 40.7 us
  Pallas kernels  39.1 us (94%)
  local copies, waits for them, and re-layouts  0.93 us (2%)
  between operations  0.64 us (2%)
    pallas_call x1, Pallas kernels, shards(): pl.pallas_call(functools.partial(kernel, n, n_lon, hp, band), out_shape=p...  39.1 us
    squeeze x1, local copies, waits for them, and re-layouts, shards(): return (both[0], both[1])  0.93 us

profile of v1, /device:TPU:0, one launch (start us, length us, event | category | flops | bytes accessed | tf_op | source)
XLA Modules:
  0.0 40.7 jit_solution(1981035588010691369)
XLA Ops:
  0.6 39.1 %panorama.1 = bf16[2,8,16,1536]{3,2,1,0:T(8,128)(2,1)S(1)} custom-call(bf16[8,16,1536]{2,1,0:T(8,128)(2,1)} %q_ref.1, bf16[8,16,1536]{2,1,0:T(8,128)(2,1)} %k_ref.1, bf16[8,16,1536]{2,1,0:T(8,128)(2,1)} %v_ref.1, bf16[8,16,1536]{2,1,0:T(8,128)(2,1)} %qt_ref.1, bf16[8,16,1536]{2,1,0:T(8,128)(2,1)} %kt_ref.1, bf16[8,16,1536]{2,1,0:T(8,128)(2,1)} %vt_ref.1, ...), custom_call_target="tpu_custom_call" | custom-call | tf_op jit(solution)/shard_map/panorama/pallas_call | solution.py:471
  39.8 0.9 %slice_bitcast_fusion = (bf16[8,16,1536]{2,1,0:T(8,128)(2,1)}, bf16[8,16,1536]{2,1,0:T(8,128)(2,1)}) fusion(bf16[2,8,16,1536]{3,2,1,0:T(8,128)(2,1)S(1)} %panorama.1), kind=kLoop, calls=%fused_computation | loop fusion | bytes 1572864 | tf_op jit(solution)/shard_map/squeeze | solution.py:505

commit v2 on v1

--- a/solution.py
+++ b/solution.py
@@ -170,7 +170,7 @@
     q_ref, k_ref, v_ref, qt_ref, kt_ref, vt_ref, row_hbm, col_hbm,
     both_ref,
     raw_kv, raw_q, kvb, hs, outs, turn, bias, row_tab, col_tab,
-    kv_send, kv_recv, q_send, q_recv, in_loc, q_loc, h_send, h_recv, o_send, o_recv, o_loc, t_loc, greet,
+    kv_send, kv_recv, q_send, q_recv, h_send, h_recv, o_send, o_recv, t_loc, greet,
 ):
     me = lax.axis_index("lat")
     lon = lax.axis_index("lon")
@@ -220,6 +220,9 @@
     q_refs = (q_ref, qt_ref)
     parts = ((0, 1), (1, hp - 1)) if hp > 1 else ((0, 1),)
 
+    def taken(ref, sem):
+        pltpu.make_async_copy(ref, ref, sem).wait()
+
     def lanes(owner, j, count):
         return pl.ds(pl.multiple_of((owner * hp + j) * HD, HD), count * HD)
 
@@ -229,8 +232,8 @@
         return pltpu.make_async_remote_copy(
             src_ref=kv_refs[a].at[:, :, lanes(peer, j, count)],
             dst_ref=raw_kv.at[a, pl.ds(me * band, band), :, j * HD:(j + count) * HD],
-            send_sem=kv_send.at[a, p, d - 1],
-            recv_sem=kv_recv.at[a, p, d - 1],
+            send_sem=kv_send,
+            recv_sem=kv_recv.at[p, a],
             device_id=(peer, lon),
             device_id_type=MESH,
         )
@@ -240,8 +243,8 @@
         return pltpu.make_async_remote_copy(
             src_ref=q_refs[a].at[:, :, lanes(peer, j, 1)],
             dst_ref=raw_q.at[j, a, pl.ds(me * band, band)],
-            send_sem=q_send.at[j, a, d - 1],
-            recv_sem=q_recv.at[j, a, d - 1],
+            send_sem=q_send,
+            recv_sem=q_recv.at[j],
             device_id=(peer, lon),
             device_id_type=MESH,
         )
@@ -250,7 +253,7 @@
         return pltpu.make_async_copy(
             q_refs[a].at[:, :, lanes(me, j, 1)],
             raw_q.at[j, a, pl.ds(me * band, band)],
-            q_loc.at[j, a],
+            q_recv.at[j],
         )
 
     def own_copy(a, p):
@@ -258,7 +261,7 @@
         return pltpu.make_async_copy(
             kv_refs[a].at[:, :, lanes(me, j, count)],
             raw_kv.at[a, pl.ds(me * band, band), :, j * HD:(j + count) * HD],
-            in_loc.at[a, p],
+            kv_recv.at[p, a],
         )
 
     halos = [(0, slice(0, 4))] + [(p, slice(a, a + 1)) for p in range(1, len(parts)) for a in range(4)]
@@ -269,8 +272,8 @@
         return pltpu.make_async_remote_copy(
             src_ref=hs.at[side, arrays, j:j + count],
             dst_ref=kvb.at[arrays, j:j + count, :, 3 - side],
-            send_sem=h_send.at[h, side],
-            recv_sem=h_recv.at[h, side],
+            send_sem=h_send,
+            recv_sem=h_recv.at[p],
             device_id=(me, right if side else left),
             device_id_type=MESH,
         )
@@ -280,8 +283,8 @@
         return pltpu.make_async_remote_copy(
             src_ref=outs.at[j, :, pl.ds(peer * band, band)],
             dst_ref=both_ref.at[:, :, :, lanes(me, j, 1)],
-            send_sem=o_send.at[j, d - 1],
-            recv_sem=o_recv.at[j, d - 1],
+            send_sem=o_send,
+            recv_sem=o_recv,
             device_id=(peer, lon),
             device_id_type=MESH,
         )
@@ -290,7 +293,7 @@
         return pltpu.make_async_copy(
             outs.at[j, :, pl.ds(me * band, band)],
             both_ref.at[:, :, :, lanes(me, j, 1)],
-            o_loc.at[j],
+            o_recv,
         )
 
     here = pl.ds(pl.multiple_of(lon * cols, cols), cols)
@@ -359,9 +362,8 @@
 
     for p in range(len(parts)):
         for a in range(4):
-            own_copy(a, p).wait()
-            for d in range(1, n):
-                kv_copy(a, p, d).wait_recv()
+            j, count = parts[p]
+            taken(raw_kv.at[a, :, :, j * HD:(j + count) * HD], kv_recv.at[p, a])
             if parts[p][1] == 1:
                 stage(a, parts[p][0])
             else:
@@ -379,15 +381,10 @@
         for p in range(len(parts)):
             @pl.when(j == parts[p][0])
             def _():
-                for h in range(len(halos)):
-                    if halos[h][0] == p:
-                        for side in range(2):
-                            halo_copy(side, h).wait_recv()
-
+                taken(kvb.at[:, parts[p][0]:sum(parts[p]), :, 2:4], h_recv.at[p])
+
+        taken(raw_q.at[j], q_recv.at[j])
         for a in range(2):
-            own_q(a, j).wait()
-            for d in range(1, n):
-                q_copy(a, j, d).wait_recv()
             raw_q[j, a] = turned(raw_q[j, a]).astype(BF).reshape(total, cols, HD)
         nq = band * cols
         for b in range(n):
@@ -434,19 +431,11 @@
             def _():
                 out_copy(j, lax.rem(b - me + n, n)).start()
 
-    for p in range(len(parts)):
-        for d in range(1, n):
-            for a in range(4):
-                kv_copy(a, p, d).wait_send()
-    for h in range(len(halos)):
-        for side in range(2):
-            halo_copy(side, h).wait_send()
-    for j in range(hp):
-        own_out(j).wait()
-        for d in range(1, n):
-            for a in range(2):
-                q_copy(a, j, d).wait_send()
-            out_copy(j, d).wait()
+    taken(raw_kv.at[:, 0:total - band], kv_send)
+    taken(raw_q.at[:, :, 0:total - band], q_send)
+    taken(hs, h_send)
+    taken(outs.at[:, :, 0:total - band], o_send)
+    taken(both_ref, o_recv)
 
 
 def shards(mesh_shape, *args):
@@ -483,17 +472,14 @@
             pltpu.VMEM((nq, nk), F32),
             pltpu.VMEM((2, total, HD), F32),
             pltpu.VMEM((2, cols, HD), F32),
-            dma((4, 2, n - 1)),
-            dma((4, 2, n - 1)),
-            dma((hp, 2, n - 1)),
-            dma((hp, 2, n - 1)),
-            dma((4, 2)),
-            dma((hp, 2)),
-            dma((5, 2)),
-            dma((5, 2)),
-            dma((hp, n - 1)),
-            dma((hp, n - 1)),
+            dma,
+            dma((2, 4)),
+            dma,
             dma((hp,)),
+            dma,
+            dma((2,)),
+            dma,
+            dma,
             dma((2,)),
             pltpu.SemaphoreType.REGULAR,
         ],

time: 41.5 us -> 40.4 us (0.973); the launches traced: 40.7 us -> 40.1 us
  Pallas kernels: 39.1 us -> 38.5 us
    pallas_call x1, Pallas kernels: 39.1 us -> 38.5 us  [shards(): pl.pallas_call(functools.partial(kernel, n, n_lon, hp, band), out_shape=p...]
where the time goes in v2:
time: 40.4 us; the launch traced here: 40.1 us
  Pallas kernels  38.5 us (95%)
  local copies, waits for them, and re-layouts  0.93 us (2%)
  between operations  0.64 us (2%)
    pallas_call x1, Pallas kernels, shards(): pl.pallas_call(functools.partial(kernel, n, n_lon, hp, band), out_shape=p...  38.5 us
    squeeze x1, local copies, waits for them, and re-layouts, shards(): return (both[0], both[1])  0.93 us

profile of v2, /device:TPU:0, one launch (start us, length us, event | category | flops | bytes accessed | tf_op | source)
XLA Modules:
  0.0 40.1 jit_solution(8468126745125950052)
XLA Ops:
  0.6 38.5 %panorama.1 = bf16[2,8,16,1536]{3,2,1,0:T(8,128)(2,1)S(1)} custom-call(bf16[8,16,1536]{2,1,0:T(8,128)(2,1)} %q_ref.1, bf16[8,16,1536]{2,1,0:T(8,128)(2,1)} %k_ref.1, bf16[8,16,1536]{2,1,0:T(8,128)(2,1)} %v_ref.1, bf16[8,16,1536]{2,1,0:T(8,128)(2,1)} %qt_ref.1, bf16[8,16,1536]{2,1,0:T(8,128)(2,1)} %kt_ref.1, bf16[8,16,1536]{2,1,0:T(8,128)(2,1)} %vt_ref.1, ...), custom_call_target="tpu_custom_call" | custom-call | tf_op jit(solution)/shard_map/panorama/pallas_call | solution.py:460
  39.2 0.9 %slice_bitcast_fusion = (bf16[8,16,1536]{2,1,0:T(8,128)(2,1)}, bf16[8,16,1536]{2,1,0:T(8,128)(2,1)}) fusion(bf16[2,8,16,1536]{3,2,1,0:T(8,128)(2,1)S(1)} %panorama.1), kind=kLoop, calls=%fused_computation | loop fusion | bytes 1572864 | tf_op jit(solution)/shard_map/squeeze | solution.py:491

commit v3 on v2

--- a/solution.py
+++ b/solution.py
@@ -170,7 +170,7 @@
     q_ref, k_ref, v_ref, qt_ref, kt_ref, vt_ref, row_hbm, col_hbm,
     both_ref,
     raw_kv, raw_q, kvb, hs, outs, turn, bias, row_tab, col_tab,
-    kv_send, kv_recv, q_send, q_recv, h_send, h_recv, o_send, o_recv, t_loc, greet,
+    kv_send, kv_recv, q_send, q_recv, h_send, h_recv, o_send, o_recv, t_loc, greet, near, peers,
 ):
     me = lax.axis_index("lat")
     lon = lax.axis_index("lon")
@@ -180,45 +180,39 @@
     total = n * band
     pairs = total // 2
 
+    def told(sem, lat, sector):
+        pl.semaphore_signal(sem, inc=1, device_id=(lat, sector), device_id_type=MESH)
+
     barrier = pltpu.get_barrier_semaphore()
-    for d in range(1, n):
-        pl.semaphore_signal(barrier, inc=1, device_id=(lax.rem(me + d, n), lon), device_id_type=MESH)
-
-    def tell(sem, side):
-        pl.semaphore_signal(sem, inc=1, device_id=(me, side), device_id_type=MESH)
-
+    lead, late = me == 0, me == n - 1
+    middle = jnp.logical_not(jnp.logical_or(lead, late))
     first, last = lon == 0, lon == n_lon - 1
     odd = lax.rem(lon, 2) == 1
     middle_odd = jnp.logical_and(odd, jnp.logical_not(last))
     middle_even = jnp.logical_and(jnp.logical_not(odd), jnp.logical_not(first))
 
-    @pl.when(middle_odd)
-    def _():
-        tell(barrier, left)
-        tell(barrier, right)
-        pl.semaphore_wait(barrier, n - 1)
-
-    @pl.when(middle_even)
-    def _():
-        pl.semaphore_wait(barrier, n + 1)
-        tell(greet, left)
-        tell(greet, right)
-
-    @pl.when(first)
-    def _():
-        tell(barrier, left)
-        pl.semaphore_wait(barrier, n)
-        tell(greet, right)
-
-    @pl.when(last)
-    def _():
-        tell(barrier, left)
-        pl.semaphore_wait(barrier, n)
-        tell(greet, right)
+    @pl.when(lead)
+    def _():
+        for d in range(1, n):
+            told(barrier, d, lon)
+
+    @pl.when(middle)
+    def _():
+        told(barrier, 0, lon)
+        told(barrier, n - 1, lon)
+
+    @pl.when(jnp.logical_and(lead, jnp.logical_or(odd, first)))
+    def _():
+        told(barrier, me, left)
+
+    @pl.when(jnp.logical_and(lead, middle_odd))
+    def _():
+        told(barrier, me, right)
 
     kv_refs = (k_ref, kt_ref, v_ref, vt_ref)
     q_refs = (q_ref, qt_ref)
-    parts = ((0, 1), (1, hp - 1)) if hp > 1 else ((0, 1),)
+    parts = tuple((j, 1) for j in range(hp))
+    order = (0, *range(n - 2, 0, -1), n - 1)
 
     def taken(ref, sem):
         pltpu.make_async_copy(ref, ref, sem).wait()
@@ -226,8 +220,7 @@
     def lanes(owner, j, count):
         return pl.ds(pl.multiple_of((owner * hp + j) * HD, HD), count * HD)
 
-    def kv_copy(a, p, d):
-        peer = lax.rem(me + d, n)
+    def kv_copy(a, p, peer):
         j, count = parts[p]
         return pltpu.make_async_remote_copy(
             src_ref=kv_refs[a].at[:, :, lanes(peer, j, count)],
@@ -238,8 +231,7 @@
             device_id_type=MESH,
         )
 
-    def q_copy(a, j, d):
-        peer = lax.rem(me + d, n)
+    def q_copy(a, j, peer):
         return pltpu.make_async_remote_copy(
             src_ref=q_refs[a].at[:, :, lanes(peer, j, 1)],
             dst_ref=raw_q.at[j, a, pl.ds(me * band, band)],
@@ -264,7 +256,7 @@
             kv_recv.at[p, a],
         )
 
-    halos = [(0, slice(0, 4))] + [(p, slice(a, a + 1)) for p in range(1, len(parts)) for a in range(4)]
+    halos = [(p, slice(0, 4)) for p in range(hp - 1)] + [(hp - 1, slice(a, a + 1)) for a in range(4)]
 
     def halo_copy(side, h):
         p, arrays = halos[h]
@@ -301,16 +293,82 @@
     col_copy = pltpu.make_async_copy(col_hbm.at[:, here], col_tab, t_loc.at[1])
     row_copy.start()
     col_copy.start()
-    for p in range(len(parts)):
+
+    @pl.when(late)
+    def _():
+        pl.semaphore_wait(barrier, n - 1)
+        for d in range(n - 1):
+            told(peers, d, lon)
+
+    @pl.when(middle)
+    def _():
+        pl.semaphore_wait(barrier, 1)
+
+    @pl.when(jnp.logical_and(lead, middle_odd))
+    def _():
+        pl.semaphore_wait(barrier, n - 2)
+
+    @pl.when(jnp.logical_and(lead, middle_even))
+    def _():
+        pl.semaphore_wait(barrier, n)
+
+    @pl.when(jnp.logical_and(lead, jnp.logical_or(first, last)))
+    def _():
+        pl.semaphore_wait(barrier, n - 1)
+
+    @pl.when(jnp.logical_not(lead))
+    def _():
         for a in range(4):
-            for d in range(1, n):
-                kv_copy(a, p, d).start()
+            kv_copy(a, 0, 0).start()
+
+    @pl.when(lead)
+    def _():
+        for d in range(1, n - 1):
+            for a in range(4):
+                kv_copy(a, 0, d).start()
+
+    @pl.when(jnp.logical_not(late))
+    def _():
+        pl.semaphore_wait(peers, 1)
+
+    @pl.when(jnp.logical_and(lead, middle_even))
+    def _():
+        told(near.at[1], me, left)
+        told(near.at[0], me, right)
+
+    @pl.when(jnp.logical_and(lead, jnp.logical_or(first, last)))
+    def _():
+        told(near.at[0], me, right)
+
+    @pl.when(lead)
+    def _():
+        for a in range(4):
+            kv_copy(a, 0, n - 1).start()
+
+    for peer in order[1:]:
+        @pl.when(jnp.logical_not(jnp.logical_or(lead, peer == me)))
+        def _():
+            for a in range(4):
+                kv_copy(a, 0, peer).start()
+
+    for a in range(4):
+        own_copy(a, 0).start()
+    for p in range(1, len(parts)):
+        for peer in order:
+            @pl.when(peer != me)
+            def _():
+                for a in range(4):
+                    kv_copy(a, p, peer).start()
+
         for a in range(4):
             own_copy(a, p).start()
     for j in range(hp):
-        for a in range(2):
-            for d in range(1, n):
-                q_copy(a, j, d).start()
+        for peer in order:
+            @pl.when(peer != me)
+            def _():
+                for a in range(2):
+                    q_copy(a, j, peer).start()
+
         for a in range(2):
             own_q(a, j).start()
 
@@ -352,13 +410,26 @@
         for side in range(2):
             hs[side, a, j] = halves[:, side].reshape(pairs, cols, HD).astype(BF)
 
-    @pl.when(middle_odd)
-    def _():
-        pl.semaphore_wait(greet, 2)
-
-    @pl.when(jnp.logical_or(first, last))
-    def _():
-        pl.semaphore_wait(greet, 1)
+    @pl.when(lead)
+    def _():
+        pl.semaphore_wait(near.at[0], 1)
+
+        @pl.when(jnp.logical_or(middle_odd, last))
+        def _():
+            told(near.at[1], me, left)
+
+        pl.semaphore_wait(near.at[1], 1)
+
+        @pl.when(middle_odd)
+        def _():
+            told(near.at[0], me, right)
+
+        @pl.when(first)
+        def _():
+            told(near.at[1], me, left)
+
+        for d in range(1, n):
+            told(greet, lax.rem(me + d, n), lon)
 
     for p in range(len(parts)):
         for a in range(4):
@@ -368,6 +439,11 @@
                 stage(a, parts[p][0])
             else:
                 pl.loop(parts[p][0], sum(parts[p]))(functools.partial(stage, a))
+            if p == 0 and a == 0:
+                @pl.when(jnp.logical_not(lead))
+                def _():
+                    pl.semaphore_wait(greet, 1)
+
             for h in range(len(halos)):
                 if halos[h][0] == p and halos[h][1].stop == a + 1:
                     for side in range(2):
@@ -387,7 +463,7 @@
         for a in range(2):
             raw_q[j, a] = turned(raw_q[j, a]).astype(BF).reshape(total, cols, HD)
         nq = band * cols
-        for b in range(n):
+        for b in order:
             first = max(0, b * band - WIN // 2)
             last = min(total, (b + 1) * band + WIN // 2)
             skip = (first - (b * band - WIN // 2)) // 2 * 64
@@ -473,14 +549,16 @@
             pltpu.VMEM((2, total, HD), F32),
             pltpu.VMEM((2, cols, HD), F32),
             dma,
-            dma((2, 4)),
+            dma((hp, 4)),
             dma,
             dma((hp,)),
             dma,
-            dma((2,)),
+            dma((hp,)),
             dma,
             dma,
             dma((2,)),
+            pltpu.SemaphoreType.REGULAR,
+            pltpu.SemaphoreType.REGULAR((2,)),
             pltpu.SemaphoreType.REGULAR,
         ],
         compiler_params=pltpu.CompilerParams(

time: 40.4 us -> 40.1 us (level)
  no operation moved by 1% of the time
where the time goes in v3:
time: 40.1 us; the launch traced here: 40 us
  Pallas kernels  38.4 us (96%)
  local copies, waits for them, and re-layouts  0.93 us (2%)
  between operations  0.64 us (2%)
    pallas_call x1, Pallas kernels, shards(): pl.pallas_call(functools.partial(kernel, n, n_lon, hp, band), out_shape=p...  38.4 us
    squeeze x1, local copies, waits for them, and re-layouts, shards(): return (both[0], both[1])  0.93 us

profile of v3, /device:TPU:0, one launch (start us, length us, event | category | flops | bytes accessed | tf_op | source)
XLA Modules:
  0.0 40.0 jit_solution(3542547994234273581)
XLA Ops:
  0.6 38.4 %panorama.1 = bf16[2,8,16,1536]{3,2,1,0:T(8,128)(2,1)S(1)} custom-call(bf16[8,16,1536]{2,1,0:T(8,128)(2,1)} %q_ref.1, bf16[8,16,1536]{2,1,0:T(8,128)(2,1)} %k_ref.1, bf16[8,16,1536]{2,1,0:T(8,128)(2,1)} %v_ref.1, bf16[8,16,1536]{2,1,0:T(8,128)(2,1)} %qt_ref.1, bf16[8,16,1536]{2,1,0:T(8,128)(2,1)} %kt_ref.1, bf16[8,16,1536]{2,1,0:T(8,128)(2,1)} %vt_ref.1, ...), custom_call_target="tpu_custom_call" | custom-call | tf_op jit(solution)/shard_map/panorama/pallas_call | solution.py:536
  39.0 0.9 %slice_bitcast_fusion = (bf16[8,16,1536]{2,1,0:T(8,128)(2,1)}, bf16[8,16,1536]{2,1,0:T(8,128)(2,1)}) fusion(bf16[2,8,16,1536]{3,2,1,0:T(8,128)(2,1)S(1)} %panorama.1), kind=kLoop, calls=%fused_computation | loop fusion | bytes 1572864 | tf_op jit(solution)/shard_map/squeeze | solution.py:569

commit v4 on v3

--- a/solution.py
+++ b/solution.py
@@ -288,6 +288,15 @@
             o_recv,
         )
 
+    def send_out(j, b):
+        @pl.when(me == b)
+        def _():
+            own_out(j).start()
+
+        @pl.when(me != b)
+        def _():
+            out_copy(j, lax.rem(b - me + n, n)).start()
+
     here = pl.ds(pl.multiple_of(lon * cols, cols), cols)
     row_copy = pltpu.make_async_copy(row_hbm, row_tab, t_loc.at[0])
     col_copy = pltpu.make_async_copy(col_hbm.at[:, here], col_tab, t_loc.at[1])
@@ -499,13 +508,14 @@
             outs[j, 0, rows] = both[:, :HD].astype(BF).reshape(band, cols, HD)
             outs[j, 1, rows] = tan.astype(BF).reshape(band, cols, HD)
 
-            @pl.when(me == b)
+            @pl.when(jnp.logical_not(odd))
             def _():
-                own_out(j).start()
-
-            @pl.when(me != b)
-            def _():
-                out_copy(j, lax.rem(b - me + n, n)).start()
+                send_out(j, b)
+
+        @pl.when(odd)
+        def _():
+            for b in order:
+                send_out(j, b)
 
     taken(raw_kv.at[:, 0:total - band], kv_send)
     taken(raw_q.at[:, :, 0:total - band], q_send)

time: 40.1 us -> 39.5 us (0.985)
  Pallas kernels: 38.4 us -> 37.8 us
    pallas_call x1, Pallas kernels: 38.4 us -> 37.8 us  [shards(): pl.pallas_call(functools.partial(kernel, n, n_lon, hp, band), out_shape=p...]
where the time goes in v4:
time: 39.5 us; the launch traced here: 39.3 us
  Pallas kernels  37.8 us (96%)
  local copies, waits for them, and re-layouts  0.93 us (2%)
  between operations  0.64 us (2%)
    pallas_call x1, Pallas kernels, shards(): pl.pallas_call(functools.partial(kernel, n, n_lon, hp, band), out_shape=p...  37.8 us
    squeeze x1, local copies, waits for them, and re-layouts, shards(): return (both[0], both[1])  0.93 us

profile of v4, /device:TPU:0, one launch (start us, length us, event | category | flops | bytes accessed | tf_op | source)
XLA Modules:
  0.0 39.3 jit_solution(7008659694269865839)
XLA Ops:
  0.6 37.8 %panorama.1 = bf16[2,8,16,1536]{3,2,1,0:T(8,128)(2,1)S(1)} custom-call(bf16[8,16,1536]{2,1,0:T(8,128)(2,1)} %q_ref.1, bf16[8,16,1536]{2,1,0:T(8,128)(2,1)} %k_ref.1, bf16[8,16,1536]{2,1,0:T(8,128)(2,1)} %v_ref.1, bf16[8,16,1536]{2,1,0:T(8,128)(2,1)} %qt_ref.1, bf16[8,16,1536]{2,1,0:T(8,128)(2,1)} %kt_ref.1, bf16[8,16,1536]{2,1,0:T(8,128)(2,1)} %vt_ref.1, ...), custom_call_target="tpu_custom_call" | custom-call | tf_op jit(solution)/shard_map/panorama/pallas_call | solution.py:546
  38.4 0.9 %slice_bitcast_fusion = (bf16[8,16,1536]{2,1,0:T(8,128)(2,1)}, bf16[8,16,1536]{2,1,0:T(8,128)(2,1)}) fusion(bf16[2,8,16,1536]{3,2,1,0:T(8,128)(2,1)S(1)} %panorama.1), kind=kLoop, calls=%fused_computation | loop fusion | bytes 1572864 | tf_op jit(solution)/shard_map/squeeze | solution.py:579

commit v5 on v4

--- a/solution.py
+++ b/solution.py
@@ -522,6 +522,17 @@
     taken(hs, h_send)
     taken(outs.at[:, :, 0:total - band], o_send)
     taken(both_ref, o_recv)
+
+
+def spread(both_ref, out_ref, tan_ref, sems):
+    copies = [
+        pltpu.make_async_copy(both_ref.at[o], ref, sems.at[o])
+        for o, ref in enumerate((out_ref, tan_ref))
+    ]
+    for copy in copies:
+        copy.start()
+    for copy in copies:
+        copy.wait()
 
 
 def shards(mesh_shape, *args):
@@ -576,7 +587,16 @@
         ),
         name="panorama",
     )(q, k, v, qt, kt, vt, jnp.asarray(row_tab), jnp.asarray(col_tab))
-    return both[0], both[1]
+    return tuple(
+        pl.pallas_call(
+            spread,
+            out_shape=[jax.ShapeDtypeStruct((band, cols, width), BF)] * 2,
+            in_specs=[anywhere],
+            out_specs=[hbm] * 2,
+            scratch_shapes=[dma((2,))],
+            name="spread",
+        )(pltpu.with_memory_space_constraint(both, pltpu.VMEM))
+    )
 
 
 def solution(mesh):

time: 39.5 us -> 39.4 us (level)
  local copies, waits for them, and re-layouts: 0.93 us -> 0 us
  Pallas kernels: 37.8 us -> 38.6 us
    squeeze x1 -> x0, local copies, waits for them, and re-layouts: 0.93 us -> none  [shards(): return (both[0], both[1])]
    pallas_call x0 -> x1, Pallas kernels: none -> 0.89 us  [shards(): pl.pallas_call(spread, out_shape=[jax.ShapeDtypeStruct((band, cols, width...]
where the time goes in v5:
time: 39.4 us; the launch traced here: 39.3 us
  Pallas kernels  38.6 us (98%)
  between operations  0.64 us (2%)
    pallas_call x1, Pallas kernels, shards(): pl.pallas_call(functools.partial(kernel, n, n_lon, hp, band), out_shape=p...  37.8 us
    pallas_call x1, Pallas kernels, shards(): pl.pallas_call(spread, out_shape=[jax.ShapeDtypeStruct((band, cols, width...  0.89 us

profile of v5, /device:TPU:0, one launch (start us, length us, event | category | flops | bytes accessed | tf_op | source)
XLA Modules:
  0.0 39.3 jit_solution(8166191892875963038)
XLA Ops:
  0.6 37.8 %panorama.1.both_ref = bf16[2,8,16,1536]{3,2,1,0:T(8,128)(2,1)S(1)} custom-call(bf16[8,16,1536]{2,1,0:T(8,128)(2,1)} %q_ref.1, bf16[8,16,1536]{2,1,0:T(8,128)(2,1)} %k_ref.1, bf16[8,16,1536]{2,1,0:T(8,128)(2,1)} %v_ref.1, bf16[8,16,1536]{2,1,0:T(8,128)(2,1)} %qt_ref.1, bf16[8,16,1536]{2,1,0:T(8,128)(2,1)} %kt_ref.1, bf16[8,16,1536]{2,1,0:T(8,128)(2,1)} %vt_ref.1, ...), custom_call_target="tpu_custom_call" | custom-call | tf_op jit(solution)/shard_map/panorama/pallas_call | solution.py:557
  38.4 0.9 %spread.1 = (bf16[8,16,1536]{2,1,0:T(8,128)(2,1)}, bf16[8,16,1536]{2,1,0:T(8,128)(2,1)}) custom-call(bf16[2,8,16,1536]{3,2,1,0:T(8,128)(2,1)S(1)} %panorama.1.both_ref), custom_call_target="tpu_custom_call" | custom-call | tf_op jit(solution)/shard_map/spread/pallas_call | solution.py:591

commit v6 on v5

--- a/solution.py
+++ b/solution.py
@@ -372,11 +372,12 @@
         for a in range(4):
             own_copy(a, p).start()
     for j in range(hp):
-        for peer in order:
-            @pl.when(peer != me)
-            def _():
-                for a in range(2):
-                    q_copy(a, j, peer).start()
+        for which, peers_in_turn in ((0, order), (1, (0, *range(1, n)))):
+            for peer in peers_in_turn:
+                @pl.when(jnp.logical_and(peer != me, lax.rem(lon, 2) == which))
+                def _():
+                    for a in range(2):
+                        q_copy(a, j, peer).start()
 
         for a in range(2):
             own_q(a, j).start()

time: 39.4 us -> 39.5 us (level)
  no operation moved by 1% of the time
where the time goes in v6:
time: 39.5 us; the launch traced here: 39.3 us
  Pallas kernels  38.7 us (98%)
  between operations  0.64 us (2%)
    pallas_call x1, Pallas kernels, shards(): pl.pallas_call(functools.partial(kernel, n, n_lon, hp, band), out_shape=p...  37.8 us
    pallas_call x1, Pallas kernels, shards(): pl.pallas_call(spread, out_shape=[jax.ShapeDtypeStruct((band, cols, width...  0.89 us

profile of v6, /device:TPU:0, one launch (start us, length us, event | category | flops | bytes accessed | tf_op | source)
XLA Modules:
  0.0 39.3 jit_solution(15911086356110199783)
XLA Ops:
  0.6 37.8 %panorama.1.both_ref = bf16[2,8,16,1536]{3,2,1,0:T(8,128)(2,1)S(1)} custom-call(bf16[8,16,1536]{2,1,0:T(8,128)(2,1)} %q_ref.1, bf16[8,16,1536]{2,1,0:T(8,128)(2,1)} %k_ref.1, bf16[8,16,1536]{2,1,0:T(8,128)(2,1)} %v_ref.1, bf16[8,16,1536]{2,1,0:T(8,128)(2,1)} %qt_ref.1, bf16[8,16,1536]{2,1,0:T(8,128)(2,1)} %kt_ref.1, bf16[8,16,1536]{2,1,0:T(8,128)(2,1)} %vt_ref.1, ...), custom_call_target="tpu_custom_call" | custom-call | tf_op jit(solution)/shard_map/panorama/pallas_call | solution.py:558
  38.4 0.9 %spread.1 = (bf16[8,16,1536]{2,1,0:T(8,128)(2,1)}, bf16[8,16,1536]{2,1,0:T(8,128)(2,1)}) custom-call(bf16[2,8,16,1536]{3,2,1,0:T(8,128)(2,1)S(1)} %panorama.1.both_ref), custom_call_target="tpu_custom_call" | custom-call | tf_op jit(solution)/shard_map/spread/pallas_call | solution.py:592

commit v7 on v5

--- a/solution.py
+++ b/solution.py
@@ -226,7 +226,7 @@
             src_ref=kv_refs[a].at[:, :, lanes(peer, j, count)],
             dst_ref=raw_kv.at[a, pl.ds(me * band, band), :, j * HD:(j + count) * HD],
             send_sem=kv_send,
-            recv_sem=kv_recv.at[p, a],
+            recv_sem=kv_recv.at[p if p < hp - 1 else p + a],
             device_id=(peer, lon),
             device_id_type=MESH,
         )
@@ -253,7 +253,7 @@
         return pltpu.make_async_copy(
             kv_refs[a].at[:, :, lanes(me, j, count)],
             raw_kv.at[a, pl.ds(me * band, band), :, j * HD:(j + count) * HD],
-            kv_recv.at[p, a],
+            kv_recv.at[p if p < hp - 1 else p + a],
         )
 
     halos = [(p, slice(0, 4)) for p in range(hp - 1)] + [(hp - 1, slice(a, a + 1)) for a in range(4)]
@@ -443,7 +443,10 @@
     for p in range(len(parts)):
         for a in range(4):
             j, count = parts[p]
-            taken(raw_kv.at[a, :, :, j * HD:(j + count) * HD], kv_recv.at[p, a])
+            if p == hp - 1:
+                taken(raw_kv.at[a, :, :, j * HD:(j + count) * HD], kv_recv.at[p + a])
+            elif a == 0:
+                taken(raw_kv.at[:, :, :, j * HD:(j + count) * HD], kv_recv.at[p])
             if parts[p][1] == 1:
                 stage(a, parts[p][0])
             else:
@@ -472,6 +475,7 @@
         for a in range(2):
             raw_q[j, a] = turned(raw_q[j, a]).astype(BF).reshape(total, cols, HD)
         nq = band * cols
+        held = jnp.logical_and(jnp.logical_and(odd, j == hp - 1), jnp.logical_not(lead))
         for b in order:
             first = max(0, b * band - WIN // 2)
             last = min(total, (b + 1) * band + WIN // 2)
@@ -508,11 +512,11 @@
             outs[j, 0, rows] = both[:, :HD].astype(BF).reshape(band, cols, HD)
             outs[j, 1, rows] = tan.astype(BF).reshape(band, cols, HD)
 
-            @pl.when(jnp.logical_not(odd))
+            @pl.when(jnp.logical_not(held))
             def _():
                 send_out(j, b)
 
-        @pl.when(odd)
+        @pl.when(held)
         def _():
             for b in order:
                 send_out(j, b)
@@ -570,7 +574,7 @@
             pltpu.VMEM((2, total, HD), F32),
             pltpu.VMEM((2, cols, HD), F32),
             dma,
-            dma((hp, 4)),
+            dma((hp + 3,)),
             dma,
             dma((hp,)),
             dma,

time: 39.4 us -> 39.5 us (level); the launches traced: 39.3 us -> 38.7 us
  Pallas kernels: 38.6 us -> 38.1 us
    pallas_call x1, Pallas kernels: 37.8 us -> 37.2 us  [shards(): pl.pallas_call(functools.partial(kernel, n, n_lon, hp, band), out_shape=p...]
where the time goes in v7:
time: 39.5 us; the launch traced here: 38.7 us
  Pallas kernels  38.1 us (96%)
  between operations  0.64 us (2%)
    pallas_call x1, Pallas kernels, shards(): pl.pallas_call(functools.partial(kernel, n, n_lon, hp, band), out_shape=p...  37.2 us
    pallas_call x1, Pallas kernels, shards(): pl.pallas_call(spread, out_shape=[jax.ShapeDtypeStruct((band, cols, width...  0.89 us

profile of v7, /device:TPU:0, one launch (start us, length us, event | category | flops | bytes accessed | tf_op | source)
XLA Modules:
  0.0 38.7 jit_solution(8303835213037387909)
XLA Ops:
  0.6 37.2 %panorama.1.both_ref = bf16[2,8,16,1536]{3,2,1,0:T(8,128)(2,1)S(1)} custom-call(bf16[8,16,1536]{2,1,0:T(8,128)(2,1)} %q_ref.1, bf16[8,16,1536]{2,1,0:T(8,128)(2,1)} %k_ref.1, bf16[8,16,1536]{2,1,0:T(8,128)(2,1)} %v_ref.1, bf16[8,16,1536]{2,1,0:T(8,128)(2,1)} %qt_ref.1, bf16[8,16,1536]{2,1,0:T(8,128)(2,1)} %kt_ref.1, bf16[8,16,1536]{2,1,0:T(8,128)(2,1)} %vt_ref.1, ...), custom_call_target="tpu_custom_call" | custom-call | tf_op jit(solution)/shard_map/panorama/pallas_call | solution.py:561
  37.8 0.9 %spread.1 = (bf16[8,16,1536]{2,1,0:T(8,128)(2,1)}, bf16[8,16,1536]{2,1,0:T(8,128)(2,1)}) custom-call(bf16[2,8,16,1536]{3,2,1,0:T(8,128)(2,1)S(1)} %panorama.1.both_ref), custom_call_target="tpu_custom_call" | custom-call | tf_op jit(solution)/shard_map/spread/pallas_call | solution.py:595
